TPU v7x, 32 devices: a whole 2x2x4 slice. The times are simulated.
32 devices in a mesh: wedge: 4 (over y, x), box: 8 (over z, core).
Axes of the slice: x: 2, y: 2, z: 4, core: 2. Of those that a mesh axis runs over, the one named last changes fastest.
Arguments:
- densities: bfloat16 [256, 4, 128], P('box', 'wedge'), may hold values from -6 to 6
- up_ops: bfloat16 [96, 128, 128], replicated, may hold values from -0.5 to 0.5
- trans_ops: bfloat16 [16, 128, 128], replicated, may hold values from -0.125 to 0.125
- down_ops: bfloat16 [96, 128, 128], replicated, may hold values from -0.0546875 to 0.0546875
- read_table: int32 [8, 128], P('box'), may hold values from 0 to 255, as said below
- interaction: int32 [256, 96, 16], P('box', 'wedge'), may hold values from 0 to 127
Outputs:
- potentials: bfloat16 [256, 4, 128], P('box', 'wedge')
Inputs may be any that keep to these rules, and one draw needn't show every extreme that they name: `read_table`: row r holds, for each box group o in order, 16 distinct boxes owned by box group o, numbered o * 32 to o * 32 + 31. interaction[b, w, k] indexes row b // 32 of read_table.
All inputs are finite; a program needn't handle non-finite values.
Results may differ from a plain program's by a relative error of at most 0.0057.
Values may be sent and summed in bfloat16 or wider, within the bound.
A program may use at most 128 MiB of HBM per device.

v0:
```python
import jax
import jax.numpy as jnp
from jax import lax
from jax.sharding import PartitionSpec as P


def body(densities, up_ops, trans_ops, down_ops, read_table, interaction):
    boxes_here = densities.shape[0]
    fields_here = densities.shape[1]
    points = densities.shape[2]
    wedge_count = up_ops.shape[0]
    coeffs = up_ops.shape[1]
    wedge_groups = lax.axis_size("wedge")
    box_groups = lax.axis_size("box")
    wedge_here = wedge_count // wedge_groups
    fields = fields_here * wedge_groups
    read_count = read_table.shape[1]
    per_owner = read_count // box_groups
    wedge_first = lax.axis_index("wedge") * wedge_here
    first_box = lax.axis_index("box") * boxes_here
    up_here = lax.dynamic_slice_in_dim(up_ops, wedge_first, wedge_here, 0)
    wanted = lax.all_to_all(
        read_table.reshape(box_groups, per_owner), "box", split_axis=0, concat_axis=0, tiled=True
    )
    local_ids = wanted - first_box
    picked = densities[local_ids]
    arrived = lax.all_to_all(picked, "box", split_axis=0, concat_axis=0, tiled=True)
    arrived = arrived.reshape(read_count, fields_here, points)
    all_fields = lax.all_gather(arrived, "wedge", axis=1, tiled=True)
    fetched = jnp.einsum(
        "sfp,wcp->swfc", all_fields, up_here, preferred_element_type=jnp.float32
    ).astype(jnp.bfloat16)
    fetched_flat = fetched.reshape(read_count, wedge_here, fields * coeffs)
    list_len = interaction.shape[2]
    by_wedge = interaction.transpose(1, 0, 2).reshape(wedge_here, boxes_here * list_len)
    slot_ids = jnp.arange(read_count, dtype=jnp.int32)
    selector = (by_wedge[:, :, None] == slot_ids[None, None, :]).astype(jnp.bfloat16)
    sources = jnp.einsum(
        "wnr,rwx->wnx", selector, fetched_flat, preferred_element_type=jnp.float32
    ).astype(jnp.bfloat16)
    sources = sources.reshape(wedge_here, boxes_here, list_len, fields, coeffs)
    local_coeffs = jnp.einsum(
        "wbkfc,kdc->wbfd", sources, trans_ops, preferred_element_type=jnp.float32
    ).astype(jnp.bfloat16)
    arrived_back = lax.all_to_all(local_coeffs, "wedge", split_axis=2, concat_axis=0, tiled=True)
    potentials = jnp.einsum(
        "wbfc,wpc->bfp", arrived_back, down_ops, preferred_element_type=jnp.float32
    )
    return potentials.astype(jnp.bfloat16)


def solution(mesh):
    in_specs = (P("box", "wedge", None), P(), P(), P(), P("box", None), P("box", "wedge", None))
    out_specs = P("box", "wedge", None)
    return jax.shard_map(body, mesh=mesh, in_specs=in_specs, out_specs=out_specs, check_vma=False)
```

profile of v0, /device:TPU:0, one launch (start us, length us, event | category | flops | bytes accessed | tf_op | source)
XLA Modules:
  0.0 88.0 jit_solution(13514578501890305852)
XLA Ops:
  0.0 0.0 copy-start
  0.0 0.5 broadcast.30
  0.5 1.6 %reduce.3 = s32[128]{0:T(128)S(1)} reduce(s32[1,128]{1,0:T(1,128)} %param.10, s32[]{:T(128)} %broadcast.30), dimensions={0}, to_apply=%param.10.reduce_sub_computation.3 | reduce | bytes 1028 | tf_op args[4]
  2.1 0.7 all_to_all.20
  2.8 6.3 %all-to-all-start = ((s32[8,1,16]{2,1,0:T(1,128)}), s32[8,1,16]{2,1,0:T(1,128)S(1)}, u32[]{:S(2)}, u32[]{:S(2)}) async-start(s32[8,1,16]{2,1,0:T(1,128)} %bitcast.4), calls=%async_computation | async-start | bytes 8192 | tf_op jit(solution)/shard_map/all_to_all | solution.py:22
  9.1 5.5 %all-to-all-done = s32[8,1,16]{2,1,0:T(1,128)S(1)} async-done(((s32[8,1,16]{2,1,0:T(1,128)}), s32[8,1,16]{2,1,0:T(1,128)S(1)}, u32[]{:S(2)}, u32[]{:S(2)}) %all-to-all-start) | async-done | bytes 544 | tf_op jit(solution)/shard_map/all_to_all | solution.py:22
  14.6 0.1 reshape.49
  14.7 1.9 %gather_fusion = bf16[128,128]{1,0:T(8,128)(2,1)} fusion(bf16[32,128]{1,0:T(8,128)(2,1)} %bitcast.48, s32[1024]{0:T(1024)S(1)} %pad_clamp_fusion), kind=kCustom, calls=%fused_computation | custom fusion | bytes 66048 | tf_op jit(solution)/shard_map/gather | solution.py:26
  16.6 3.9 %all-to-all-start.1 = ((bf16[8,16,1,128]{3,1,2,0:T(8,128)(2,1)}), bf16[8,16,1,128]{3,1,2,0:T(8,128)(2,1)}, u32[]{:S(2)}, u32[]{:S(2)}) async-start(bf16[8,16,1,128]{3,1,2,0:T(8,128)(2,1)} %bitcast.8), calls=%async_computation.1 | async-start | bytes 65536 | tf_op jit(solution)/shard_map/all_to_all | solution.py:27
  20.6 1.1 %copy.13 = s32[24,32,16]{2,1,0:T(8,128)S(1)} copy(s32[24,32,16]{1,2,0:T(8,128)} %bitcast.50) | data formatting | bytes 98304 | tf_op jit(solution)/shard_map/transpose | solution.py:35
  21.7 0.8 eq.15
  22.5 3.8 %all-to-all-done.1 = bf16[8,16,1,128]{3,1,2,0:T(8,128)(2,1)} async-done(((bf16[8,16,1,128]{3,1,2,0:T(8,128)(2,1)}), bf16[8,16,1,128]{3,1,2,0:T(8,128)(2,1)}, u32[]{:S(2)}, u32[]{:S(2)}) %all-to-all-start.1) | async-done | bytes 32800 | tf_op jit(solution)/shard_map/all_to_all | solution.py:27
  26.3 8.7 %all_gather.3 = bf16[128,4,128]{2,0,1:T(8,128)(2,1)S(1)} all-gather(bf16[128,1,128]{2,0,1:T(8,128)(2,1)} %bitcast.9), channel_id=1, replica_groups=mesh['wedge'=4,'box'=8] {'wedge'}, dimensions={1}, use_global_device_ids=true | all-gather | bytes 163840 | tf_op jit(solution)/shard_map/all_gather | solution.py:29
  35.0 0.0 copy-done
  35.0 1.0 %convolution_convert_fusion.1 = bf16[24,128,128,4]{2,1,3,0:T(8,128)(2,1)S(1)} fusion(bf16[96,128,128]{2,1,0:T(8,128)(2,1)S(1)} %copy-done, s32[]{:T(128)S(6)} %select_n.13, bf16[128,4,128]{2,0,1:T(8,128)(2,1)S(1)} %all_gather.3), kind=kOutput, calls=%fused_computation.6 | convolution fusion | flops 404226048 | bytes 4063236 | tf_op jit(solution)/shard_map/sfp,wcp->swfc/dot_general | solution.py:30
  36.0 0.0 copy-done.2
  36.0 6.4 %convolution_convert_fusion = bf16[24,512,512]{2,1,0:T(8,128)(2,1)} fusion(bf16[128,24,512]{0,2,1:T(8,128)(2,1)S(1)} %bitcast.47, s32[24,512]{1,0:T(8,128)S(1)} %copy-done.2), kind=kOutput, calls=%fused_computation.3 | convolution fusion | flops 1618477056 | bytes 15777792 | tf_op jit(solution)/shard_map/wnr,rwx->wnx/dot_general | solution.py:38
  42.4 18.2 %reshape.43 = bf16[24,32,16,4,128]{4,3,2,1,0:T(4,128)(2,1)} reshape(bf16[24,512,512]{2,1,0:T(8,128)(2,1)} %convolution_convert_fusion) | data formatting | bytes 25165824 | tf_op jit(solution)/shard_map/reshape | solution.py:41
  60.6 13.2 %bitcast_convert_fusion = bf16[24,32,4,128]{3,1,2,0:T(8,128)(2,1)S(1)} fusion(bf16[24,32,16,4,128]{4,3,2,1,0:T(4,128)(2,1)} %reshape.43, bf16[16,128,128]{2,1,0:T(8,128)(2,1)} %param.8), kind=kOutput, calls=%fused_computation.7 | convolution fusion | flops 1611005952 | bytes 13893632 | tf_op jit(solution)/shard_map/wbkfc,kdc->wbfd/dot_general | solution.py:42
  73.7 0.0 copy-start.1
  73.8 0.1 copy.19
  73.8 12.5 %all_to_all.29 = bf16[24,32,4,128]{3,1,0,2:T(8,128)(2,1)S(1)} all-to-all(bf16[24,32,4,128]{3,1,0,2:T(8,128)(2,1)S(1)} %copy.19), channel_id=1, replica_groups=mesh['wedge'=4,'box'=8] {'wedge'}, dimensions={2} | all-to-all | bytes 1572864 | tf_op jit(solution)/shard_map/all_to_all | solution.py:45
  86.3 0.0 copy-done.1
  86.3 1.7 %fusion.6 = bf16[32,1,128]{2,0,1:T(8,128)(2,1)} fusion(bf16[96,32,128]{2,1,0:T(8,128)(2,1)S(1)} %bitcast.49, bf16[96,128,128]{2,1,0:T(8,128)(2,1)S(1)} %copy-done.1), kind=kOutput, calls=%fused_computation.10 | convolution fusion | flops 100667392 | bytes 3940352 | tf_op jit(solution)/shard_map/wbfc,wpc->bfp/dot_general | solution.py:46
  (3 shorter events, 0.0 us)
Async XLA Ops:
  0.0 35.0 %copy-start = (bf16[96,128,128]{2,1,0:T(8,128)(2,1)S(1)}, bf16[96,128,128]{2,1,0:T(8,128)(2,1)}, u32[]{:S(2)}) copy-start(bf16[96,128,128]{2,1,0:T(8,128)(2,1)} %param.7) | copy-start | bytes 9437188
  2.8 11.8 %all-to-all-start = ((s32[8,1,16]{2,1,0:T(1,128)}), s32[8,1,16]{2,1,0:T(1,128)S(1)}, u32[]{:S(2)}, u32[]{:S(2)}) async-start(s32[8,1,16]{2,1,0:T(1,128)} %bitcast.4), calls=%async_computation | async-start | bytes 8192 | tf_op jit(solution)/shard_map/all_to_all | solution.py:22
  16.6 9.7 %all-to-all-start.1 = ((bf16[8,16,1,128]{3,1,2,0:T(8,128)(2,1)}), bf16[8,16,1,128]{3,1,2,0:T(8,128)(2,1)}, u32[]{:S(2)}, u32[]{:S(2)}) async-start(bf16[8,16,1,128]{3,1,2,0:T(8,128)(2,1)} %bitcast.8), calls=%async_computation.1 | async-start | bytes 65536 | tf_op jit(solution)/shard_map/all_to_all | solution.py:27
  22.5 13.5 %copy-start.2 = (s32[24,512]{1,0:T(8,128)S(1)}, s32[24,512]{1,0:T(8,128)}, u32[]{:S(2)}) copy-start(s32[24,512]{1,0:T(8,128)} %eq.15) | copy-start | bytes 147460
  73.7 12.5 %copy-start.1 = (bf16[96,128,128]{2,1,0:T(8,128)(2,1)S(1)}, bf16[96,128,128]{2,1,0:T(8,128)(2,1)}, u32[]{:S(2)}) copy-start(bf16[96,128,128]{2,1,0:T(8,128)(2,1)} %param.9) | copy-start | bytes 9437188
where the time goes:
time: 88.8 us; the launch traced here: 88 us
  local copies, waits for them, and re-layouts  23.4 us (26%)
  matrix products  22.3 us (25%)
  blocking collectives  21.1 us (24%)
  starting transfers between devices  10.3 us (12%)
  waiting for transfers between devices  9.29 us (10%)
  other arithmetic  1.58 us (2%)
    reshape x1, local copies, waits for them, and re-layouts, body(): sources = sources.reshape(wedge_here, boxes_here, list_len, fields, coeffs)  18.2 us
    dot_general x1, matrix products, body(): jnp.einsum('wbkfc,kdc->wbfd', sources, trans_ops, preferred_element_type=...  13.2 us
    all_to_all x1, blocking collectives, body(): lax.all_to_all(local_coeffs, 'wedge', split_axis=2, concat_axis=0, tiled=...  12.5 us
    all_gather x1, blocking collectives, body(): all_fields = lax.all_gather(arrived, 'wedge', axis=1, tiled=True)  8.66 us
    dot_general x1, matrix products, body(): jnp.einsum('wnr,rwx->wnx', selector, fetched_flat, preferred_element_type...  6.44 us
    all_to_all x1, starting transfers between devices, body(): lax.all_to_all(read_table.reshape(box_groups, per_owner), 'box', split_ax...  6.33 us
    all_to_all x1, waiting for transfers between devices, body(): lax.all_to_all(read_table.reshape(box_groups, per_owner), 'box', split_ax...  5.48 us
    all_to_all x1, starting transfers between devices, body(): lax.all_to_all(picked, 'box', split_axis=0, concat_axis=0, tiled=True)  3.94 us
  transfers between devices with their start and end apart: 2, of which 2 were waited for; matrix products, arithmetic and copies ran while one was open for 2% of the time, Pallas kernels for 0%

commit v1 on v0

v1 whole, which is shorter than its diff:
```python
import functools

import jax
import jax.numpy as jnp
from jax import lax
from jax.experimental import pallas as pl
from jax.experimental.pallas import tpu as pltpu
from jax.sharding import PartitionSpec as P

MESH = pl.DeviceIdType.MESH
F32 = jnp.float32
BF16 = jnp.bfloat16


def kernel(
    wedge_groups, box_groups, list_len, group,
    dens_ref, up_ref, trans_ref, down_ref, table_ref, inter_ref, out_ref,
    up_in, trans_in, down_in, table_in, inter_in,
    all_boxes, slots, up_t, trans_t, down_t, select, picked, equiv, total, arrived,
    load_sem, box_send, box_recv, slot_send, slot_recv, part_send, part_recv,
):
    boxes, points = dens_ref.shape
    wedges, coeffs = up_in.shape[0], up_in.shape[1]
    reads = table_ref.shape[1]
    fields = wedge_groups
    me_w = lax.axis_index("wedge")
    me_b = lax.axis_index("box")
    first = me_w * wedges
    my_rows = pl.ds(pl.multiple_of(me_b * boxes, boxes), boxes)

    loads = [
        pltpu.make_async_copy(dens_ref, all_boxes.at[my_rows], load_sem.at[0]),
        pltpu.make_async_copy(table_ref, table_in, load_sem.at[1]),
        pltpu.make_async_copy(inter_ref, inter_in, load_sem.at[2]),
        pltpu.make_async_copy(trans_ref, trans_in, load_sem.at[3]),
        pltpu.make_async_copy(up_ref.at[pl.ds(first, wedges)], up_in, load_sem.at[4]),
        pltpu.make_async_copy(down_ref.at[pl.ds(first, wedges)], down_in, load_sem.at[5]),
    ]

    barrier = pltpu.get_barrier_semaphore()
    for off in range(1, box_groups):
        pl.semaphore_signal(
            barrier, inc=1, device_id={"box": lax.rem(me_b + off, box_groups)}, device_id_type=MESH
        )
    for off in range(1, wedge_groups):
        pl.semaphore_signal(
            barrier, inc=1, device_id={"wedge": lax.rem(me_w + off, wedge_groups)}, device_id_type=MESH
        )
    for load in loads:
        load.start()
    pl.semaphore_wait(barrier, box_groups + wedge_groups - 2)

    box_copies = []
    for off in range(1, box_groups):
        copy = pltpu.make_async_remote_copy(
            src_ref=dens_ref,
            dst_ref=all_boxes.at[my_rows],
            send_sem=box_send.at[off],
            recv_sem=box_recv.at[off],
            device_id={"box": lax.rem(me_b + off, box_groups)},
            device_id_type=MESH,
        )
        copy.start()
        box_copies.append(copy)

    loads[1].wait()
    loads[2].wait()
    lanes = lax.broadcasted_iota(jnp.int32, (boxes, reads), 1)
    per_chunk = 128 // list_len

    def build(chunk, carry):
        rows = inter_in[pl.ds(pl.multiple_of(chunk * 128, 128), 128), :]
        columns = rows.T
        for j in range(per_chunk):
            for k in range(list_len):
                at = j * list_len + k
                hot = (columns[:, at:at + 1] == lanes).astype(F32).astype(BF16)
                select[chunk * per_chunk + j, k * boxes:(k + 1) * boxes, :] = hot
        return carry

    lax.fori_loop(0, wedges // per_chunk, build, 0)

    table_col = jnp.broadcast_to(table_in[...], (reads, reads)).T
    own = lax.broadcasted_iota(jnp.int32, (reads, reads), 1)

    loads[0].wait()
    for off in range(1, box_groups):
        source = lax.rem(me_b - off + box_groups, box_groups)
        rows = pl.ds(pl.multiple_of(source * boxes, boxes), boxes)
        pltpu.make_async_remote_copy(
            src_ref=dens_ref,
            dst_ref=all_boxes.at[rows],
            send_sem=box_send.at[off],
            recv_sem=box_recv.at[off],
            device_id={"box": source},
            device_id_type=MESH,
        ).wait_recv()

    chosen = jnp.zeros((reads, points), F32)
    for tile in range(all_boxes.shape[0] // reads):
        hot = (table_col == own + tile * reads).astype(F32).astype(BF16)
        chosen = chosen + jnp.dot(
            hot, all_boxes[tile * reads:(tile + 1) * reads, :], preferred_element_type=F32
        )
    slots[me_w] = chosen.astype(BF16)

    slot_copies = []
    for off in range(1, wedge_groups):
        copy = pltpu.make_async_remote_copy(
            src_ref=slots.at[me_w],
            dst_ref=slots.at[me_w],
            send_sem=slot_send.at[off],
            recv_sem=slot_recv.at[off],
            device_id={"wedge": lax.rem(me_w + off, wedge_groups)},
            device_id_type=MESH,
        )
        copy.start()
        slot_copies.append(copy)

    for load in loads[3:]:
        load.wait()

    def turn_trans(k, carry):
        trans_t[pl.ds(pl.multiple_of(k * coeffs, coeffs), coeffs), :] = trans_in[k].T
        return carry

    lax.fori_loop(0, list_len, turn_trans, 0)

    def turn_maps(pair, carry):
        for half in range(2):
            w = 2 * pair + half
            up_t[pair, :, half * coeffs:(half + 1) * coeffs] = up_in[w].T
            down_t[pl.ds(pl.multiple_of(w * coeffs, coeffs), coeffs), :] = down_in[w].T
        return carry

    lax.fori_loop(0, wedges // 2, turn_maps, 0)

    total[...] = jnp.zeros_like(total)
    for off in range(1, wedge_groups):
        source = lax.rem(me_w - off + wedge_groups, wedge_groups)
        pltpu.make_async_remote_copy(
            src_ref=slots.at[source],
            dst_ref=slots.at[source],
            send_sem=slot_send.at[off],
            recv_sem=slot_recv.at[off],
            device_id={"wedge": source},
            device_id_type=MESH,
        ).wait_recv()

    def work(step, carry):
        all_slots = slots[...].reshape(fields * reads, points)
        for pair in range(group // 2):
            both = jnp.dot(
                all_slots, up_t[step * (group // 2) + pair], preferred_element_type=F32
            ).astype(BF16)
            for half in range(2):
                for f in range(fields):
                    equiv[2 * pair + half, :, f * coeffs:(f + 1) * coeffs] = both[
                        f * reads:(f + 1) * reads, half * coeffs:(half + 1) * coeffs
                    ]
        for i in range(group):
            got = jnp.dot(
                select[step * group + i], equiv[i], preferred_element_type=F32
            ).astype(BF16)
            for k in range(list_len):
                for f in range(fields):
                    row = (i * fields + f) * boxes
                    picked[row:row + boxes, k * coeffs:(k + 1) * coeffs] = got[
                        k * boxes:(k + 1) * boxes, f * coeffs:(f + 1) * coeffs
                    ]
        local = jnp.dot(picked[...], trans_t[...], preferred_element_type=F32).astype(BF16)
        rows = fields * boxes
        wide = jnp.concatenate([local[i * rows:(i + 1) * rows] for i in range(group)], axis=1)
        span = group * coeffs
        total[...] += jnp.dot(
            wide, down_t[pl.ds(pl.multiple_of(step * span, span), span), :],
            preferred_element_type=F32,
        )
        return carry

    lax.fori_loop(0, wedges // group, work, 0)

    part_copies = []
    for off in range(1, wedge_groups):
        peer = lax.rem(me_w + off, wedge_groups)
        copy = pltpu.make_async_remote_copy(
            src_ref=total.at[pl.ds(pl.multiple_of(peer * boxes, boxes), boxes)],
            dst_ref=arrived.at[off - 1],
            send_sem=part_send.at[off],
            recv_sem=part_recv.at[off],
            device_id={"wedge": peer},
            device_id_type=MESH,
        )
        copy.start()
        part_copies.append(copy)
    for copy in box_copies + slot_copies:
        copy.wait_send()
    result = total[pl.ds(pl.multiple_of(me_w * boxes, boxes), boxes), :]
    for off, copy in enumerate(part_copies):
        copy.wait_recv()
        result = result + arrived[off]
    out_ref[...] = result.astype(BF16)
    for copy in part_copies:
        copy.wait_send()


def body(densities, up_ops, trans_ops, down_ops, read_table, interaction):
    boxes, _, points = densities.shape
    coeffs = up_ops.shape[1]
    wedge_groups = lax.axis_size("wedge")
    box_groups = lax.axis_size("box")
    wedges = up_ops.shape[0] // wedge_groups
    list_len = interaction.shape[2]
    reads = read_table.shape[1]
    fields = wedge_groups
    group = 4
    lists = interaction.transpose(1, 2, 0).reshape(wedges * list_len, boxes)
    anywhere = pl.BlockSpec(memory_space=pl.ANY)
    flops = 2 * wedges * fields * coeffs * (
        reads * points + boxes * list_len * (reads + coeffs) + boxes * points
    )
    result = pl.pallas_call(
        functools.partial(kernel, wedge_groups, box_groups, list_len, group),
        out_shape=jax.ShapeDtypeStruct((boxes, points), BF16),
        in_specs=[anywhere] * 6,
        out_specs=pl.BlockSpec(memory_space=pltpu.VMEM),
        scratch_shapes=[
            pltpu.VMEM((wedges, coeffs, points), BF16),
            pltpu.VMEM((list_len, coeffs, coeffs), BF16),
            pltpu.VMEM((wedges, points, coeffs), BF16),
            pltpu.VMEM((1, reads), jnp.int32),
            pltpu.VMEM((wedges * list_len, boxes), jnp.int32),
            pltpu.VMEM((box_groups * boxes, points), BF16),
            pltpu.VMEM((fields, reads, points), BF16),
            pltpu.VMEM((wedges // 2, points, 2 * coeffs), BF16),
            pltpu.VMEM((list_len * coeffs, coeffs), BF16),
            pltpu.VMEM((wedges * coeffs, points), BF16),
            pltpu.VMEM((wedges, list_len * boxes, reads), BF16),
            pltpu.VMEM((group * fields * boxes, list_len * coeffs), BF16),
            pltpu.VMEM((group, reads, fields * coeffs), BF16),
            pltpu.VMEM((fields * boxes, points), F32),
            pltpu.VMEM((wedge_groups - 1, boxes, points), F32),
            pltpu.SemaphoreType.DMA((6,)),
            pltpu.SemaphoreType.DMA((box_groups,)),
            pltpu.SemaphoreType.DMA((box_groups,)),
            pltpu.SemaphoreType.DMA((wedge_groups,)),
            pltpu.SemaphoreType.DMA((wedge_groups,)),
            pltpu.SemaphoreType.DMA((wedge_groups,)),
            pltpu.SemaphoreType.DMA((wedge_groups,)),
        ],
        compiler_params=pltpu.CompilerParams(
            collective_id=0, has_side_effects=True, vmem_limit_bytes=48 * 1024 * 1024
        ),
        cost_estimate=pl.CostEstimate(flops=flops, bytes_accessed=3 << 20, transcendentals=0),
    )(densities.reshape(boxes, points), up_ops, trans_ops, down_ops, read_table, lists)
    return result.reshape(boxes, 1, points)


def solution(mesh):
    in_specs = (P("box", "wedge", None), P(), P(), P(), P("box", None), P("box", "wedge", None))
    out_specs = P("box", "wedge", None)
    return jax.shard_map(body, mesh=mesh, in_specs=in_specs, out_specs=out_specs, check_vma=False)
```

time: 88.8 us -> 37.5 us (0.42)
  Pallas kernels: 0 us -> 31.4 us
  matrix products: 22.3 us -> 0 us
  blocking collectives: 21.1 us -> 0 us
  local copies, waits for them, and re-layouts: 23.4 us -> 5.81 us
  starting transfers between devices: 10.3 us -> 0 us
  waiting for transfers between devices: 9.29 us -> 0 us
  other arithmetic: 1.58 us -> 0 us
    pallas_call x0 -> x1, Pallas kernels: none -> 31.4 us  [body(): pl.pallas_call(functools.partial(kernel, wedge_groups, box_groups, list_l...]
    dot_general x4 -> x0, matrix products: 22.3 us -> none  [the longest x1 13.2 us: body(): jnp.einsum('wbkfc,kdc->wbfd', sources, trans_ops, preferred_element_type=...]
    reshape x1 -> x0, local copies, waits for them, and re-layouts: 18.2 us -> none  [body(): sources = sources.reshape(wedge_here, boxes_here, list_len, fields, coeffs)]
    all_to_all x1 -> x0, blocking collectives: 12.5 us -> none  [body(): lax.all_to_all(local_coeffs, 'wedge', split_axis=2, concat_axis=0, tiled=...]
    all_to_all x2 -> x0, starting transfers between devices: 10.3 us -> none  [the longest x1 6.33 us: body(): lax.all_to_all(read_table.reshape(box_groups, per_owner), 'box', split_ax...]
    all_to_all x2 -> x0, waiting for transfers between devices: 9.29 us -> none  [the longest x1 5.48 us: body(): lax.all_to_all(read_table.reshape(box_groups, per_owner), 'box', split_ax...]
    all_gather x1 -> x0, blocking collectives: 8.66 us -> none  [body(): all_fields = lax.all_gather(arrived, 'wedge', axis=1, tiled=True)]
    unnamed x7 -> x11, local copies, waits for them, and re-layouts: 0.52 us -> 5.81 us
  transfers between devices with their start and end apart: 2 -> 0, of which waited for: 2 -> 0; matrix products, arithmetic and copies ran while one was open for 2% -> 0% of each run, Pallas kernels for 0% -> 0%
where the time goes in v1:
time: 37.5 us; the launch traced here: 37.3 us
  Pallas kernels  31.4 us (84%)
  local copies, waits for them, and re-layouts  5.81 us (15%)
    pallas_call x1, Pallas kernels, body(): pl.pallas_call(functools.partial(kernel, wedge_groups, box_groups, list_l...  31.4 us
    unnamed x11, local copies, waits for them, and re-layouts  5.81 us

profile of v1, /device:TPU:0, one launch (start us, length us, event | category | flops | bytes accessed | tf_op | source)
XLA Modules:
  0.0 37.3 jit_solution(15520857487199336552)
XLA Ops:
  0.0 0.0 copy-start
  0.0 1.9 %copy-done = bf16[96,128,128]{2,1,0:T(8,128)(2,1)S(1)} copy-done((bf16[96,128,128]{2,1,0:T(8,128)(2,1)S(1)}, bf16[96,128,128]{2,1,0:T(8,128)(2,1)}, u32[]{:S(2)}) %copy-start) | copy-done | bytes 3145752
  1.9 0.0 copy-start.1
  1.9 1.0 %copy-done.1 = bf16[16,128,128]{2,1,0:T(8,128)(2,1)S(1)} copy-done((bf16[16,128,128]{2,1,0:T(8,128)(2,1)S(1)}, bf16[16,128,128]{2,1,0:T(8,128)(2,1)}, u32[]{:S(2)}) %copy-start.1) | copy-done | bytes 524312
  2.9 0.0 copy-start.2
  2.9 0.9 %copy-done.2 = s32[32,24,16]{0,2,1:T(8,128)S(1)} copy-done((s32[32,24,16]{0,2,1:T(8,128)S(1)}, s32[32,24,16]{0,2,1:T(8,128)}, u32[]{:S(2)}) %copy-start.2) | copy-done | bytes 49176
  3.9 0.0 copy-start.3
  3.9 0.7 %copy-done.3 = bf16[32,1,128]{2,0,1:T(8,128)(2,1)S(1)} copy-done((bf16[32,1,128]{2,0,1:T(8,128)(2,1)S(1)}, bf16[32,1,128]{2,0,1:T(8,128)(2,1)}, u32[]{:S(2)}) %copy-start.3) | copy-done | bytes 8216
  4.6 0.0 copy-start.4
  4.6 0.7 %copy-done.4 = s32[1,128]{1,0:T(1,128)S(1)} copy-done((s32[1,128]{1,0:T(1,128)S(1)}, s32[1,128]{1,0:T(1,128)}, u32[]{:S(2)}) %copy-start.4) | copy-done | bytes 536
  5.2 31.4 %shard_map.64 = bf16[32,128]{1,0:T(8,128)(2,1)S(1)} custom-call(bf16[32,128]{1,0:T(8,128)(2,1)S(1)} %bitcast.7, bf16[96,128,128]{2,1,0:T(8,128)(2,1)S(1)} %copy-done, bf16[16,128,128]{2,1,0:T(8,128)(2,1)S(1)} %copy-done.1, bf16[96,128,128]{2,1,0:T(8,128)(2,1)} %down_ref.1, s32[1,128]{1,0:T(1,128)S(1)} %copy-done.4, s32[384,32]{1,0:T(8,128)S(1)} %bitcast.6), custom_call_target="tpu_custom_call" | custom-call | flops 3724541952 | bytes 3145728 | tf_op jit(solution)/shard_map/pallas_call | solution.py:222
  36.7 0.6 %copy.8 = bf16[32,1,128]{2,0,1:T(8,128)(2,1)} copy(bf16[32,1,128]{2,0,1:T(8,128)(2,1)S(1)} %bitcast.5) | data formatting | bytes 16384
Async XLA Ops:
  0.0 1.9 %copy-start = (bf16[96,128,128]{2,1,0:T(8,128)(2,1)S(1)}, bf16[96,128,128]{2,1,0:T(8,128)(2,1)}, u32[]{:S(2)}) copy-start(bf16[96,128,128]{2,1,0:T(8,128)(2,1)} %up_ref.1) | copy-start | bytes 9437188
  1.9 1.0 %copy-start.1 = (bf16[16,128,128]{2,1,0:T(8,128)(2,1)S(1)}, bf16[16,128,128]{2,1,0:T(8,128)(2,1)}, u32[]{:S(2)}) copy-start(bf16[16,128,128]{2,1,0:T(8,128)(2,1)} %trans_ref.1) | copy-start | bytes 1572868
  2.9 0.9 %copy-start.2 = (s32[32,24,16]{0,2,1:T(8,128)S(1)}, s32[32,24,16]{0,2,1:T(8,128)}, u32[]{:S(2)}) copy-start(s32[32,24,16]{0,2,1:T(8,128)} %param.11) | copy-start | bytes 147460
  3.9 0.7 %copy-start.3 = (bf16[32,1,128]{2,0,1:T(8,128)(2,1)S(1)}, bf16[32,1,128]{2,0,1:T(8,128)(2,1)}, u32[]{:S(2)}) copy-start(bf16[32,1,128]{2,0,1:T(8,128)(2,1)} %param.6) | copy-start | bytes 24580
  4.6 0.7 %copy-start.4 = (s32[1,128]{1,0:T(1,128)S(1)}, s32[1,128]{1,0:T(1,128)}, u32[]{:S(2)}) copy-start(s32[1,128]{1,0:T(1,128)} %table_ref.1) | copy-start | bytes 1540

commit v2 on v1

--- a/solution.py
+++ b/solution.py
@@ -16,7 +16,7 @@
     wedge_groups, box_groups, list_len, group,
     dens_ref, up_ref, trans_ref, down_ref, table_ref, inter_ref, out_ref,
     up_in, trans_in, down_in, table_in, inter_in,
-    all_boxes, slots, up_t, trans_t, down_t, select, picked, equiv, total, arrived,
+    all_boxes, slots, trans_t, select, picked, equiv, total, arrived,
     load_sem, box_send, box_recv, slot_send, slot_recv, part_send, part_recv,
 ):
     boxes, points = dens_ref.shape
@@ -126,15 +126,6 @@
 
     lax.fori_loop(0, list_len, turn_trans, 0)
 
-    def turn_maps(pair, carry):
-        for half in range(2):
-            w = 2 * pair + half
-            up_t[pair, :, half * coeffs:(half + 1) * coeffs] = up_in[w].T
-            down_t[pl.ds(pl.multiple_of(w * coeffs, coeffs), coeffs), :] = down_in[w].T
-        return carry
-
-    lax.fori_loop(0, wedges // 2, turn_maps, 0)
-
     total[...] = jnp.zeros_like(total)
     for off in range(1, wedge_groups):
         source = lax.rem(me_w - off + wedge_groups, wedge_groups)
@@ -147,20 +138,25 @@
             device_id_type=MESH,
         ).wait_recv()
 
+    def outgoing(pair, carry):
+        all_slots = slots[...].reshape(fields * reads, points)
+        maps = up_in[pl.ds(2 * pair, 2)].reshape(2 * coeffs, points)
+        both = lax.dot_general(
+            all_slots, maps, (((1,), (1,)), ((), ())), preferred_element_type=F32
+        ).astype(BF16)
+        for half in range(2):
+            for f in range(fields):
+                equiv[2 * pair + half, :, f * coeffs:(f + 1) * coeffs] = both[
+                    f * reads:(f + 1) * reads, half * coeffs:(half + 1) * coeffs
+                ]
+        return carry
+
+    lax.fori_loop(0, wedges // 2, outgoing, 0)
+
     def work(step, carry):
-        all_slots = slots[...].reshape(fields * reads, points)
-        for pair in range(group // 2):
-            both = jnp.dot(
-                all_slots, up_t[step * (group // 2) + pair], preferred_element_type=F32
-            ).astype(BF16)
-            for half in range(2):
-                for f in range(fields):
-                    equiv[2 * pair + half, :, f * coeffs:(f + 1) * coeffs] = both[
-                        f * reads:(f + 1) * reads, half * coeffs:(half + 1) * coeffs
-                    ]
         for i in range(group):
             got = jnp.dot(
-                select[step * group + i], equiv[i], preferred_element_type=F32
+                select[step * group + i], equiv[step * group + i], preferred_element_type=F32
             ).astype(BF16)
             for k in range(list_len):
                 for f in range(fields):
@@ -171,10 +167,9 @@
         local = jnp.dot(picked[...], trans_t[...], preferred_element_type=F32).astype(BF16)
         rows = fields * boxes
         wide = jnp.concatenate([local[i * rows:(i + 1) * rows] for i in range(group)], axis=1)
-        span = group * coeffs
-        total[...] += jnp.dot(
-            wide, down_t[pl.ds(pl.multiple_of(step * span, span), span), :],
-            preferred_element_type=F32,
+        maps = jnp.concatenate([down_in[step * group + i] for i in range(group)], axis=1)
+        total[...] += lax.dot_general(
+            wide, maps, (((1,), (1,)), ((), ())), preferred_element_type=F32
         )
         return carry
 
@@ -213,9 +208,9 @@
     list_len = interaction.shape[2]
     reads = read_table.shape[1]
     fields = wedge_groups
-    group = 4
+    group = 8
     lists = interaction.transpose(1, 2, 0).reshape(wedges * list_len, boxes)
-    anywhere = pl.BlockSpec(memory_space=pl.ANY)
+    anywhere = pl.BlockSpec(memory_space=pltpu.HBM)
     flops = 2 * wedges * fields * coeffs * (
         reads * points + boxes * list_len * (reads + coeffs) + boxes * points
     )
@@ -232,12 +227,10 @@
             pltpu.VMEM((wedges * list_len, boxes), jnp.int32),
             pltpu.VMEM((box_groups * boxes, points), BF16),
             pltpu.VMEM((fields, reads, points), BF16),
-            pltpu.VMEM((wedges // 2, points, 2 * coeffs), BF16),
             pltpu.VMEM((list_len * coeffs, coeffs), BF16),
-            pltpu.VMEM((wedges * coeffs, points), BF16),
             pltpu.VMEM((wedges, list_len * boxes, reads), BF16),
             pltpu.VMEM((group * fields * boxes, list_len * coeffs), BF16),
-            pltpu.VMEM((group, reads, fields * coeffs), BF16),
+            pltpu.VMEM((wedges, reads, fields * coeffs), BF16),
             pltpu.VMEM((fields * boxes, points), F32),
             pltpu.VMEM((wedge_groups - 1, boxes, points), F32),
             pltpu.SemaphoreType.DMA((6,)),
@@ -249,7 +242,7 @@
             pltpu.SemaphoreType.DMA((wedge_groups,)),
         ],
         compiler_params=pltpu.CompilerParams(
-            collective_id=0, has_side_effects=True, vmem_limit_bytes=48 * 1024 * 1024
+            collective_id=0, has_side_effects=True, vmem_limit_bytes=64 * 1024 * 1024
         ),
         cost_estimate=pl.CostEstimate(flops=flops, bytes_accessed=3 << 20, transcendentals=0),
     )(densities.reshape(boxes, points), up_ops, trans_ops, down_ops, read_table, lists)

time: 37.5 us -> 29.3 us (0.78)
  local copies, waits for them, and re-layouts: 5.81 us -> 1.3 us
  Pallas kernels: 31.4 us -> 27.8 us
    unnamed x11 -> x1, local copies, waits for them, and re-layouts: 5.81 us -> 1.3 us
    pallas_call x1, Pallas kernels: 31.4 us -> 27.8 us  [body(): pl.pallas_call(functools.partial(kernel, wedge_groups, box_groups, list_l...]
where the time goes in v2:
time: 29.3 us; the launch traced here: 29.1 us
  Pallas kernels  27.8 us (95%)
  local copies, waits for them, and re-layouts  1.3 us (4%)
    pallas_call x1, Pallas kernels, body(): pl.pallas_call(functools.partial(kernel, wedge_groups, box_groups, list_l...  27.8 us
    unnamed x1, local copies, waits for them, and re-layouts  1.3 us

profile of v2, /device:TPU:0, one launch (start us, length us, event | category | flops | bytes accessed | tf_op | source)
XLA Modules:
  0.0 29.1 jit_solution(1549987632390143451)
XLA Ops:
  0.0 27.8 %shard_map.64 = bf16[32,128]{1,0:T(8,128)(2,1)} custom-call(bf16[32,128]{1,0:T(8,128)(2,1)} %bitcast.7, bf16[96,128,128]{2,1,0:T(8,128)(2,1)} %up_ref.1, bf16[16,128,128]{2,1,0:T(8,128)(2,1)} %trans_ref.1, bf16[96,128,128]{2,1,0:T(8,128)(2,1)} %down_ref.1, s32[1,128]{1,0:T(1,128)} %table_ref.1, s32[384,32]{1,0:T(8,128)} %bitcast.6), custom_call_target="tpu_custom_call" | custom-call | flops 3724541952 | bytes 3145728 | tf_op jit(solution)/shard_map/pallas_call | solution.py:217
  27.8 1.3 %copy.8 = bf16[32,1,128]{2,0,1:T(8,128)(2,1)} copy(bf16[32,1,128]{2,0,1:T(8,128)(2,1)} %bitcast.5) | data formatting | bytes 16384

commit v3 on v2

--- a/solution.py
+++ b/solution.py
@@ -16,7 +16,7 @@
     wedge_groups, box_groups, list_len, group,
     dens_ref, up_ref, trans_ref, down_ref, table_ref, inter_ref, out_ref,
     up_in, trans_in, down_in, table_in, inter_in,
-    all_boxes, slots, trans_t, select, picked, equiv, total, arrived,
+    all_boxes, slots, trans_t, select, even, odd, equiv, total, arrived,
     load_sem, box_send, box_recv, slot_send, slot_recv, part_send, part_recv,
 ):
     boxes, points = dens_ref.shape
@@ -63,6 +63,14 @@
         copy.start()
         box_copies.append(copy)
 
+    loads[3].wait()
+
+    def turn_trans(k, carry):
+        trans_t[pl.ds(pl.multiple_of(k * coeffs, coeffs), coeffs), :] = trans_in[k].T
+        return carry
+
+    lax.fori_loop(0, list_len, turn_trans, 0, unroll=4)
+
     loads[1].wait()
     loads[2].wait()
     lanes = lax.broadcasted_iota(jnp.int32, (boxes, reads), 1)
@@ -78,7 +86,7 @@
                 select[chunk * per_chunk + j, k * boxes:(k + 1) * boxes, :] = hot
         return carry
 
-    lax.fori_loop(0, wedges // per_chunk, build, 0)
+    lax.fori_loop(0, 1, build, 0)
 
     table_col = jnp.broadcast_to(table_in[...], (reads, reads)).T
     own = lax.broadcasted_iota(jnp.int32, (reads, reads), 1)
@@ -117,14 +125,9 @@
         copy.start()
         slot_copies.append(copy)
 
-    for load in loads[3:]:
-        load.wait()
-
-    def turn_trans(k, carry):
-        trans_t[pl.ds(pl.multiple_of(k * coeffs, coeffs), coeffs), :] = trans_in[k].T
-        return carry
-
-    lax.fori_loop(0, list_len, turn_trans, 0)
+    lax.fori_loop(1, wedges // per_chunk, build, 0)
+    loads[4].wait()
+    loads[5].wait()
 
     total[...] = jnp.zeros_like(total)
     for off in range(1, wedge_groups):
@@ -153,7 +156,7 @@
 
     lax.fori_loop(0, wedges // 2, outgoing, 0)
 
-    def work(step, carry):
+    def gather(step, picked):
         for i in range(group):
             got = jnp.dot(
                 select[step * group + i], equiv[step * group + i], preferred_element_type=F32
@@ -164,6 +167,8 @@
                     picked[row:row + boxes, k * coeffs:(k + 1) * coeffs] = got[
                         k * boxes:(k + 1) * boxes, f * coeffs:(f + 1) * coeffs
                     ]
+
+    def translate(step, picked):
         local = jnp.dot(picked[...], trans_t[...], preferred_element_type=F32).astype(BF16)
         rows = fields * boxes
         wide = jnp.concatenate([local[i * rows:(i + 1) * rows] for i in range(group)], axis=1)
@@ -171,9 +176,21 @@
         total[...] += lax.dot_general(
             wide, maps, (((1,), (1,)), ((), ())), preferred_element_type=F32
         )
-        return carry
-
-    lax.fori_loop(0, wedges // group, work, 0)
+
+    steps = wedges // group
+    gather(0, even)
+
+    def work(turn, carry):
+        gather(2 * turn + 1, odd)
+        translate(2 * turn, even)
+        gather(2 * turn + 2, even)
+        translate(2 * turn + 1, odd)
+        return carry
+
+    lax.fori_loop(0, steps // 2 - 1, work, 0)
+    gather(steps - 1, odd)
+    translate(steps - 2, even)
+    translate(steps - 1, odd)
 
     part_copies = []
     for off in range(1, wedge_groups):
@@ -208,7 +225,7 @@
     list_len = interaction.shape[2]
     reads = read_table.shape[1]
     fields = wedge_groups
-    group = 8
+    group = 4
     lists = interaction.transpose(1, 2, 0).reshape(wedges * list_len, boxes)
     anywhere = pl.BlockSpec(memory_space=pltpu.HBM)
     flops = 2 * wedges * fields * coeffs * (
@@ -230,6 +247,7 @@
             pltpu.VMEM((list_len * coeffs, coeffs), BF16),
             pltpu.VMEM((wedges, list_len * boxes, reads), BF16),
             pltpu.VMEM((group * fields * boxes, list_len * coeffs), BF16),
+            pltpu.VMEM((group * fields * boxes, list_len * coeffs), BF16),
             pltpu.VMEM((wedges, reads, fields * coeffs), BF16),
             pltpu.VMEM((fields * boxes, points), F32),
             pltpu.VMEM((wedge_groups - 1, boxes, points), F32),

time: 29.3 us -> 30.7 us (1.048)
  Pallas kernels: 27.8 us -> 29.2 us
    pallas_call x1, Pallas kernels: 27.8 us -> 29.2 us  [body(): pl.pallas_call(functools.partial(kernel, wedge_groups, box_groups, list_l...]
where the time goes in v3:
time: 30.7 us; the launch traced here: 30.5 us
  Pallas kernels  29.2 us (95%)
  local copies, waits for them, and re-layouts  1.3 us (4%)
    pallas_call x1, Pallas kernels, body(): pl.pallas_call(functools.partial(kernel, wedge_groups, box_groups, list_l...  29.2 us
    unnamed x1, local copies, waits for them, and re-layouts  1.3 us

profile of v3, /device:TPU:0, one launch (start us, length us, event | category | flops | bytes accessed | tf_op | source)
XLA Modules:
  0.0 30.5 jit_solution(7347753309594856586)
XLA Ops:
  0.0 29.2 %shard_map.64 = bf16[32,128]{1,0:T(8,128)(2,1)} custom-call(bf16[32,128]{1,0:T(8,128)(2,1)} %bitcast.7, bf16[96,128,128]{2,1,0:T(8,128)(2,1)} %up_ref.1, bf16[16,128,128]{2,1,0:T(8,128)(2,1)} %trans_ref.1, bf16[96,128,128]{2,1,0:T(8,128)(2,1)} %down_ref.1, s32[1,128]{1,0:T(1,128)} %table_ref.1, s32[384,32]{1,0:T(8,128)} %bitcast.6), custom_call_target="tpu_custom_call" | custom-call | flops 3724541952 | bytes 3145728 | tf_op jit(solution)/shard_map/pallas_call | solution.py:234
  29.2 1.3 %copy.8 = bf16[32,1,128]{2,0,1:T(8,128)(2,1)} copy(bf16[32,1,128]{2,0,1:T(8,128)(2,1)} %bitcast.5) | data formatting | bytes 16384

commit v4 on v2

--- a/solution.py
+++ b/solution.py
@@ -63,22 +63,27 @@
         copy.start()
         box_copies.append(copy)
 
+    loads[3].wait()
+
+    def turn_trans(k, carry):
+        trans_t[pl.ds(pl.multiple_of(k * coeffs, coeffs), coeffs), :] = trans_in[k].T
+        return carry
+
+    lax.fori_loop(0, list_len, turn_trans, 0, unroll=2)
+
     loads[1].wait()
     loads[2].wait()
     lanes = lax.broadcasted_iota(jnp.int32, (boxes, reads), 1)
-    per_chunk = 128 // list_len
-
-    def build(chunk, carry):
-        rows = inter_in[pl.ds(pl.multiple_of(chunk * 128, 128), 128), :]
-        columns = rows.T
-        for j in range(per_chunk):
-            for k in range(list_len):
-                at = j * list_len + k
-                hot = (columns[:, at:at + 1] == lanes).astype(F32).astype(BF16)
-                select[chunk * per_chunk + j, k * boxes:(k + 1) * boxes, :] = hot
-        return carry
-
-    lax.fori_loop(0, wedges // per_chunk, build, 0)
+    early = wedges // 3
+
+    def build(w, carry):
+        columns = inter_in[pl.ds(pl.multiple_of(w * list_len, list_len), list_len), :].T
+        for k in range(list_len):
+            hot = (columns[:, k:k + 1] == lanes).astype(F32).astype(BF16)
+            select[w, k * boxes:(k + 1) * boxes, :] = hot
+        return carry
+
+    lax.fori_loop(0, early, build, 0)
 
     table_col = jnp.broadcast_to(table_in[...], (reads, reads)).T
     own = lax.broadcasted_iota(jnp.int32, (reads, reads), 1)
@@ -117,14 +122,9 @@
         copy.start()
         slot_copies.append(copy)
 
-    for load in loads[3:]:
-        load.wait()
-
-    def turn_trans(k, carry):
-        trans_t[pl.ds(pl.multiple_of(k * coeffs, coeffs), coeffs), :] = trans_in[k].T
-        return carry
-
-    lax.fori_loop(0, list_len, turn_trans, 0)
+    lax.fori_loop(early, wedges, build, 0)
+    loads[4].wait()
+    loads[5].wait()
 
     total[...] = jnp.zeros_like(total)
     for off in range(1, wedge_groups):
@@ -154,16 +154,21 @@
     lax.fori_loop(0, wedges // 2, outgoing, 0)
 
     def work(step, carry):
-        for i in range(group):
-            got = jnp.dot(
-                select[step * group + i], equiv[step * group + i], preferred_element_type=F32
-            ).astype(BF16)
-            for k in range(list_len):
+        def gather(pair, carry):
+            for half in range(2):
+                i = 2 * pair + half
+                got = jnp.dot(
+                    select[step * group + i], equiv[step * group + i], preferred_element_type=F32
+                ).astype(BF16)
                 for f in range(fields):
-                    row = (i * fields + f) * boxes
-                    picked[row:row + boxes, k * coeffs:(k + 1) * coeffs] = got[
-                        k * boxes:(k + 1) * boxes, f * coeffs:(f + 1) * coeffs
-                    ]
+                    row = pl.multiple_of((i * fields + f) * boxes, boxes)
+                    for k in range(list_len):
+                        picked[pl.ds(row, boxes), k * coeffs:(k + 1) * coeffs] = got[
+                            k * boxes:(k + 1) * boxes, f * coeffs:(f + 1) * coeffs
+                        ]
+            return carry
+
+        lax.fori_loop(0, group // 2, gather, 0)
         local = jnp.dot(picked[...], trans_t[...], preferred_element_type=F32).astype(BF16)
         rows = fields * boxes
         wide = jnp.concatenate([local[i * rows:(i + 1) * rows] for i in range(group)], axis=1)

time: 29.3 us -> 32.4 us (1.11)
  Pallas kernels: 27.8 us -> 30.9 us
    pallas_call x1, Pallas kernels: 27.8 us -> 30.9 us  [body(): pl.pallas_call(functools.partial(kernel, wedge_groups, box_groups, list_l...]
where the time goes in v4:
time: 32.4 us; the launch traced here: 32.2 us
  Pallas kernels  30.9 us (95%)
  local copies, waits for them, and re-layouts  1.3 us (4%)
    pallas_call x1, Pallas kernels, body(): pl.pallas_call(functools.partial(kernel, wedge_groups, box_groups, list_l...  30.9 us
    unnamed x1, local copies, waits for them, and re-layouts  1.3 us

profile of v4, /device:TPU:0, one launch (start us, length us, event | category | flops | bytes accessed | tf_op | source)
XLA Modules:
  0.0 32.2 jit_solution(7597363213973205702)
XLA Ops:
  0.0 30.9 %shard_map.64 = bf16[32,128]{1,0:T(8,128)(2,1)} custom-call(bf16[32,128]{1,0:T(8,128)(2,1)} %bitcast.7, bf16[96,128,128]{2,1,0:T(8,128)(2,1)} %up_ref.1, bf16[16,128,128]{2,1,0:T(8,128)(2,1)} %trans_ref.1, bf16[96,128,128]{2,1,0:T(8,128)(2,1)} %down_ref.1, s32[1,128]{1,0:T(1,128)} %table_ref.1, s32[384,32]{1,0:T(8,128)} %bitcast.6), custom_call_target="tpu_custom_call" | custom-call | flops 3724541952 | bytes 3145728 | tf_op jit(solution)/shard_map/pallas_call | solution.py:222
  30.9 1.3 %copy.8 = bf16[32,1,128]{2,0,1:T(8,128)(2,1)} copy(bf16[32,1,128]{2,0,1:T(8,128)(2,1)} %bitcast.5) | data formatting | bytes 16384

commit v5 on v2

--- a/solution.py
+++ b/solution.py
@@ -124,7 +124,7 @@
         trans_t[pl.ds(pl.multiple_of(k * coeffs, coeffs), coeffs), :] = trans_in[k].T
         return carry
 
-    lax.fori_loop(0, list_len, turn_trans, 0)
+    lax.fori_loop(0, list_len, turn_trans, 0, unroll=8)
 
     total[...] = jnp.zeros_like(total)
     for off in range(1, wedge_groups):
@@ -151,7 +151,7 @@
                 ]
         return carry
 
-    lax.fori_loop(0, wedges // 2, outgoing, 0)
+    lax.fori_loop(0, wedges // 2, outgoing, 0, unroll=4)
 
     def work(step, carry):
         for i in range(group):

time: 29.3 us -> 27.8 us (0.949)
  Pallas kernels: 27.8 us -> 26.3 us
    pallas_call x1, Pallas kernels: 27.8 us -> 26.3 us  [body(): pl.pallas_call(functools.partial(kernel, wedge_groups, box_groups, list_l...]
where the time goes in v5:
time: 27.8 us; the launch traced here: 27.6 us
  Pallas kernels  26.3 us (95%)
  local copies, waits for them, and re-layouts  1.3 us (5%)
    pallas_call x1, Pallas kernels, body(): pl.pallas_call(functools.partial(kernel, wedge_groups, box_groups, list_l...  26.3 us
    unnamed x1, local copies, waits for them, and re-layouts  1.3 us

profile of v5, /device:TPU:0, one launch (start us, length us, event | category | flops | bytes accessed | tf_op | source)
XLA Modules:
  0.0 27.6 jit_solution(7252722653145434394)
XLA Ops:
  0.0 26.3 %shard_map.64 = bf16[32,128]{1,0:T(8,128)(2,1)} custom-call(bf16[32,128]{1,0:T(8,128)(2,1)} %bitcast.7, bf16[96,128,128]{2,1,0:T(8,128)(2,1)} %up_ref.1, bf16[16,128,128]{2,1,0:T(8,128)(2,1)} %trans_ref.1, bf16[96,128,128]{2,1,0:T(8,128)(2,1)} %down_ref.1, s32[1,128]{1,0:T(1,128)} %table_ref.1, s32[384,32]{1,0:T(8,128)} %bitcast.6), custom_call_target="tpu_custom_call" | custom-call | flops 3724541952 | bytes 3145728 | tf_op jit(solution)/shard_map/pallas_call | solution.py:217
  26.3 1.3 %copy.8 = bf16[32,1,128]{2,0,1:T(8,128)(2,1)} copy(bf16[32,1,128]{2,0,1:T(8,128)(2,1)} %bitcast.5) | data formatting | bytes 16384
